TPU v7x, 32 devices: a whole 2x2x4 slice. The times are simulated.
32 devices in a mesh: grp: 2 (over y), ep: 8 (over z, x), tp: 2 (over core).
Axes of the slice: x: 2, y: 2, z: 4, core: 2. Of those that a mesh axis runs over, the one named last changes fastest.
Arguments:
- cotangent: bfloat16 [2048, 3584], P(('grp', 'ep'), 'tp'), parts along dimension 0, may hold values from -1.5 to 1.5
- gate_weights: bfloat16 [2048, 8], P(('grp', 'ep')), parts along dimension 0, may hold values from 0.099609375 to 2
- expert_ids: int32 [2048, 8], P(('grp', 'ep')), parts along dimension 0, may hold values from 0 to 15, as said below
- slot_ids: int32 [2048, 8], P(('grp', 'ep')), parts along dimension 0, may hold values from 0 to 65, as said below
- pre_acts: bfloat16 [16, 1056, 2, 1024], P('ep', 'grp', None, 'tp'), parts along dimension 1, may hold values from -6 to 6
- w_down: bfloat16 [16, 1024, 3584], P('ep', 'tp'), may hold values from -0.1875 to 0.1875
Outputs:
- grad_pre: bfloat16 [16, 1056, 2, 1024], P('ep', 'grp', None, 'tp'), parts along dimension 1
- grad_gates: float32 [2048, 8], P(('grp', 'ep')), parts along dimension 0
There are 2 independent parts, one for each index of `grp`. A program takes and returns all parts, laid end to end along the dimension named above; an argument that names none is the same for every part. Nothing has to cross between parts.
Inputs may be any that keep to these rules, and one draw needn't show every extreme that they name: `expert_ids`: each token names 8 different experts; the rows of one index of ep name no expert more than 66 times, and some expert is named exactly 66 times by the rows of every index of ep. `slot_ids`: for each index of ep and each expert, the choices that name that expert have distinct positions.
All inputs are finite; a program needn't handle non-finite values.
Results may differ from a plain program's by a relative error of at most 0.001.
Values may be sent and summed in bfloat16 or wider, within the bound.
A program may use at most 128 MiB of HBM per device.

v0:
```python
import jax
import jax.numpy as jnp
from jax import lax
from jax.sharding import PartitionSpec as P


def shards(cotangent, gate_weights, expert_ids, slot_ids, pre_acts, w_down):
    peers = lax.axis_size("ep")
    tok_rows, chosen = expert_ids.shape
    experts_here = w_down.shape[0]
    slot_rows = pre_acts.shape[1]
    capacity = slot_rows // peers
    owners = expert_ids // experts_here
    target_slot = expert_ids % experts_here * slot_rows + owners * capacity + slot_ids
    pair_index = jnp.arange(tok_rows * chosen, dtype=jnp.int32)
    filler = (
        jnp.full((experts_here * slot_rows,), tok_rows * chosen, jnp.int32)
        .at[target_slot.reshape(-1)]
        .set(pair_index)
    )
    padded_gate = jnp.concatenate(
        [gate_weights.reshape(-1), jnp.zeros((1,), gate_weights.dtype)], axis=0
    )
    send_gate = padded_gate[filler].reshape(experts_here, peers, capacity)
    padded = jnp.concatenate(
        [cotangent, jnp.zeros((1, cotangent.shape[1]), cotangent.dtype)], axis=0
    )
    half_rows = lax.all_to_all(
        padded[filler // chosen].reshape(experts_here, peers, capacity, cotangent.shape[1]),
        "ep",
        split_axis=1,
        concat_axis=1,
        tiled=True,
    )
    arrived_gate = lax.all_to_all(send_gate, "ep", split_axis=1, concat_axis=1, tiled=True)
    arrived = lax.all_gather(half_rows, "tp", axis=3, tiled=True)
    arrived = arrived.reshape(experts_here, slot_rows, arrived.shape[3])
    gate_rows = arrived_gate.reshape(experts_here, slot_rows).astype(jnp.float32)
    grad_hidden = jnp.einsum("esd,ehd->esh", arrived, w_down, preferred_element_type=jnp.float32)
    gate_pre = pre_acts[:, :, 0].astype(jnp.float32)
    up_pre = pre_acts[:, :, 1].astype(jnp.float32)
    sigmoid_gate = jax.nn.sigmoid(gate_pre)
    activated = gate_pre * sigmoid_gate
    partial_grad = jnp.sum(activated * up_pre * grad_hidden, axis=2)
    scaled = gate_rows[:, :, None] * grad_hidden
    grad_gate = scaled * up_pre * sigmoid_gate * (1.0 + gate_pre * (1.0 - sigmoid_gate))
    grad_up = scaled * activated
    grad_pre = jnp.stack([grad_gate, grad_up], axis=2).astype(jnp.bfloat16)
    partial_grad = partial_grad.reshape(experts_here, peers, capacity)
    summed = lax.psum(partial_grad, "tp")
    returned = lax.all_to_all(summed, "ep", split_axis=1, concat_axis=1, tiled=True)
    grad_gates = returned.reshape(-1)[target_slot]
    return (grad_pre, grad_gates)


def solution(mesh):
    placed = (
        P(("grp", "ep"), "tp"),
        P(("grp", "ep"), None),
        P(("grp", "ep"), None),
        P(("grp", "ep"), None),
        P("ep", "grp", None, "tp"),
        P("ep", "tp", None),
    )
    return jax.shard_map(
        shards,
        mesh=mesh,
        in_specs=placed,
        out_specs=(P("ep", "grp", None, "tp"), P(("grp", "ep"), None)),
        check_vma=False,
    )
```

profile of v0, /device:TPU:0, one launch (start us, length us, event | category | flops | bytes accessed | tf_op | source)
XLA Modules:
  0.0 180.5 jit_solution(4882719302171784767)
XLA Ops:
  7.2 0.0 all-gather.2.cloned.1.call-start
  7.2 0.7 compare_select_fusion.2
  7.9 0.1 copy.43
  8.0 0.1 reshape.66
  8.2 4.3 %scatter_custom_fusion = s32[1056]{0:T(1024)S(1)} fusion(s32[1024]{0:T(1024)S(1)} %bitcast.24, s32[1024]{0:T(1024)S(1)} %iota.3, s32[]{:T(128)} %constant.48.clone.1), kind=kCustom, calls=%fused_computation.53 | custom fusion | bytes 4228 | tf_op jit(solution)/shard_map/scatter | solution.py:19
  12.5 1.1 concatenate.7
  13.6 5.5 %gather_fusion.1 = bf16[1056,1792]{1,0:T(8,128)(2,1)} fusion(bf16[129,1792]{1,0:T(8,128)(2,1)S(1)} %concatenate.7, s32[2048]{0:T(1024)S(1)} %get-tuple-element.21), kind=kCustom, calls=%fused_computation.1 | custom fusion | bytes 7573632 | tf_op jit(solution)/shard_map/gather | solution.py:29
  19.1 5.0 %reshape.68 = bf16[2,8,66,1792]{3,2,1,0:T(8,128)(2,1)} reshape(bf16[1056,1792]{1,0:T(8,128)(2,1)} %gather_fusion.1) | data formatting | bytes 7569408 | tf_op jit(solution)/shard_map/reshape | solution.py:29
  24.1 6.1 %copy.46 = bf16[2,8,66,1792]{3,0,2,1:T(2,128)(2,1)S(1)} copy(bf16[2,8,66,1792]{3,2,1,0:T(8,128)(2,1)} %reshape.68) | data formatting | bytes 7569408 | tf_op jit(solution)/shard_map/reshape | solution.py:29
  30.1 92.0 %all_to_all.15 = bf16[2,8,66,1792]{3,0,2,1:T(2,128)(2,1)} all-to-all(bf16[2,8,66,1792]{3,0,2,1:T(2,128)(2,1)S(1)} %copy.46), channel_id=1, replica_groups=mesh['grp'=2,'ep'=8,'tp'=2] {'ep'}, dimensions={1} | all-to-all | bytes 7569408 | tf_op jit(solution)/shard_map/all_to_all | solution.py:28
  122.1 0.0 copy-start.1
  122.1 0.0 all-gather.2.cloned.1.call-update
  122.2 0.7 copy-done.1
  122.8 0.1 copy.42
  122.9 0.1 reshape.65
  123.1 0.0 copy-start
  123.1 6.9 %gather_fusion = bf16[1056]{0:T(1024)(128)(2,1)S(1)} fusion(bf16[1025]{0:T(1024)(128)(2,1)S(1)} %pad_maximum_fusion.1, s32[2048]{0:T(1024)S(1)} %get-tuple-element.22), kind=kCustom, calls=%fused_computation | custom fusion | bytes 8448 | tf_op jit(solution)/shard_map/gather | solution.py:24
  130.0 0.1 reshape.67
  130.1 0.6 copy.44
  130.7 3.5 %all-to-all-start = ((bf16[2,8,66]{2,0,1:T(2,128)(2,1)}), bf16[2,8,66]{2,0,1:T(2,128)(2,1)S(1)}, u32[]{:S(2)}, u32[]{:S(2)}) async-start(bf16[2,8,66]{2,0,1:T(2,128)(2,1)} %copy.44), calls=%async_computation | async-start | bytes 8192 | tf_op jit(solution)/shard_map/all_to_all | solution.py:35
  134.2 0.1 copy.52
  134.3 0.1 reshape.93
  134.4 0.0 copy-done
  134.4 4.2 %fusion.26 = (bf16[2,528,1,512]{3,2,1,0:T(2,128)(2,1)}, bf16[2,528,1,512]{3,2,1,0:T(2,128)(2,1)}) fusion(bf16[2,528,2,512]{3,2,1,0:T(2,128)(2,1)S(1)} %copy-done), kind=kLoop, calls=%fused_computation.58 | loop fusion | bytes 4325376 | tf_op jit(solution)/shard_map/slice | solution.py:41
  138.7 1.7 all-to-all-done
  140.4 0.1 reshape.72
  140.4 0.0 all-gather.2.cloned.1.call-done
  140.5 11.7 %fusion.6 = (f32[2,528]{1,0:T(2,128)S(1)}, bf16[2,528,1,512]{3,1,0,2:T(8,128)(2,1)S(1)}, bf16[2,528,1,512]{3,1,0,2:T(8,128)(2,1)S(1)}) fusion(bf16[2,528,1,512]{3,2,1,0:T(2,128)(2,1)} %get-tuple-element.17, bf16[2,528,1,512]{3,2,1,0:T(2,128)(2,1)} %get-tuple-element.18, f32[2,528]{1,0:T(2,128)S(1)} %reshape.72, bf16[2,512,3584]{2,1,0:T(8,128)(2,1)} %param.11, ...), kind=kOutput, calls=%fused_computation.15 | convolution fusion | flops 3885808640 | bytes 19243264 | tf_op jit(solution)/shard_map/esd,ehd->esh/dot_general | solution.py:39
  152.2 0.1 reshape.70
  152.3 2.5 %psum.7 = f32[2,8,66]{2,1,0:T(8,128)S(1)} all-reduce(f32[2,8,66]{2,1,0:T(8,128)S(1)} %reshape.70), channel_id=1, replica_groups=mesh['grp'=2,'ep'=8,'tp'=2] {'tp'}, use_global_device_ids=true, to_apply=%region_2.3 | all-reduce | flops 1056 | bytes 8448 | tf_op jit(solution)/shard_map/psum | solution.py:50
  154.8 0.6 copy.50
  155.4 4.8 %all-to-all-start.2 = ((f32[2,8,66]{2,0,1:T(2,128)}), f32[2,8,66]{2,0,1:T(2,128)S(1)}, u32[]{:S(2)}, u32[]{:S(2)}) async-start(f32[2,8,66]{2,0,1:T(2,128)} %copy.50), calls=%async_computation.2 | async-start | bytes 16384 | tf_op jit(solution)/shard_map/all_to_all | solution.py:51
  160.2 0.2 pad_maximum_fusion
  160.4 3.6 %copy.53 = bf16[2,528,2,512]{3,2,1,0:T(2,128)(2,1)} copy(bf16[2,528,2,512]{3,1,0,2:T(8,128)(2,1)S(1)} %pad_maximum_fusion) | data formatting | bytes 4325376
  163.9 2.7 %all-to-all-done.2 = f32[2,8,66]{2,0,1:T(2,128)S(1)} async-done(((f32[2,8,66]{2,0,1:T(2,128)}), f32[2,8,66]{2,0,1:T(2,128)S(1)}, u32[]{:S(2)}, u32[]{:S(2)}) %all-to-all-start.2) | async-done | bytes 4256 | tf_op jit(solution)/shard_map/all_to_all | solution.py:51
  166.7 0.1 reshape.71
  166.8 6.2 %gather_fusion.2 = f32[1024]{0:T(1024)S(1)} fusion(f32[1056]{0:T(1024)S(1)} %reshape.71, s32[1024]{0:T(1024)S(1)} %broadcast_clamp_fusion), kind=kCustom, calls=%fused_computation.2 | custom fusion | bytes 12288 | tf_op jit(solution)/shard_map/gather | solution.py:52
  172.9 0.1 reshape.92
  173.0 0.7 copy.54
  (8 shorter events, 0.0 us)
Async XLA Ops:
  7.2 133.3 %all-gather.2.cloned.1.call-start = ((), (), s32[]{:S(2)}) async-start(), calls=%async_computation.3 | async-start | bytes 11354112 | tf_op jit(solution)/shard_map/all_gather | solution.py:36
  122.1 0.7 copy-start.1
  123.1 11.3 %copy-start = (bf16[2,528,2,512]{3,2,1,0:T(2,128)(2,1)S(1)}, bf16[2,528,2,512]{3,2,1,0:T(2,128)(2,1)}, u32[]{:S(2)}) copy-start(bf16[2,528,2,512]{3,2,1,0:T(2,128)(2,1)} %param.10) | copy-start | bytes 6488068
  130.7 9.6 %all-to-all-start = ((bf16[2,8,66]{2,0,1:T(2,128)(2,1)}), bf16[2,8,66]{2,0,1:T(2,128)(2,1)S(1)}, u32[]{:S(2)}, u32[]{:S(2)}) async-start(bf16[2,8,66]{2,0,1:T(2,128)(2,1)} %copy.44), calls=%async_computation | async-start | bytes 8192 | tf_op jit(solution)/shard_map/all_to_all | solution.py:35
  155.4 11.3 %all-to-all-start.2 = ((f32[2,8,66]{2,0,1:T(2,128)}), f32[2,8,66]{2,0,1:T(2,128)S(1)}, u32[]{:S(2)}, u32[]{:S(2)}) async-start(f32[2,8,66]{2,0,1:T(2,128)} %copy.50), calls=%async_computation.2 | async-start | bytes 16384 | tf_op jit(solution)/shard_map/all_to_all | solution.py:51
Sparse Core Ops, SparseCore 0:
  122.3 17.1 all-gather.1
where the time goes:
time: 181 us
  blocking collectives  94.5 us (52%)
  local copies, waits for them, and re-layouts  46.4 us (26%)
  between operations  14.2 us (8%)
  matrix products  11.7 us (6%)
  starting transfers between devices  8.33 us (5%)
  waiting for transfers between devices  4.47 us (2%)
    all_to_all x1, blocking collectives, shards(): lax.all_to_all(padded[filler // chosen].reshape(experts_here, peers, capa...  92 us
    dot_general x1, matrix products, shards(): jnp.einsum('esd,ehd->esh', arrived, w_down, preferred_element_type=jnp.fl...  11.7 us
    reshape x2, local copies, waits for them, and re-layouts, shards(): padded[filler // chosen]  11 us
    gather x1, local copies, waits for them, and re-layouts, shards(): send_gate = padded_gate[filler].reshape(experts_here, peers, capacity)  6.92 us
    gather x2, local copies, waits for them, and re-layouts, shards(): grad_gates = returned.reshape(-1)[target_slot]  6.23 us
    gather x1, local copies, waits for them, and re-layouts, shards(): padded[filler // chosen]  5.54 us
    unnamed x7, local copies, waits for them, and re-layouts  5.01 us
    all_to_all x1, starting transfers between devices, shards(): lax.all_to_all(summed, 'ep', split_axis=1, concat_axis=1, tiled=True)  4.8 us
  transfers between devices with their start and end apart: 3, of which 2 were waited for; matrix products, arithmetic and copies ran while one was open for 9% of the time, Pallas kernels for 0%

commit v1 on v0

--- a/solution.py
+++ b/solution.py
@@ -1,10 +1,18 @@
+import functools
+
 import jax
 import jax.numpy as jnp
 from jax import lax
+from jax.experimental import pallas as pl
+from jax.experimental.pallas import tpu as pltpu
 from jax.sharding import PartitionSpec as P
 
-
-def shards(cotangent, gate_weights, expert_ids, slot_ids, pre_acts, w_down):
+MESH = pl.DeviceIdType.MESH
+KC = 256
+NZ, NX = 4, 2
+
+
+def slotted(cotangent, gate_weights, expert_ids, slot_ids, pre_acts, w_down):
     peers = lax.axis_size("ep")
     tok_rows, chosen = expert_ids.shape
     experts_here = w_down.shape[0]
@@ -53,6 +61,480 @@
     return (grad_pre, grad_gates)
 
 
+def kernel(
+    dims,
+    x_ref, eid_ref, slot_ref, gate_ref, pre_ref, w_ref,
+    out_ref, gg_ref,
+    buf, wv, prev, outv, tmp, coef, grad, onehot, meta, mysend, rsend, rrecv,
+    own_recv, tp_recv, z_send, x_send, tp_send, loc_sem, w_sem, pre_sem, out_sem,
+    m_send, m_recv, r_send, r_recv,
+):
+    experts, slots, cap, hid, chunks = dims
+    m = NX * cap
+    mp = onehot.shape[1]
+    cbs = hid // 128
+    per = 2 * cbs
+    unit = m * per
+    me = lax.axis_index("ep")
+    t = lax.axis_index("tp")
+    z, x = me // NX, me % NX
+    oz = 1 - x
+    last = chunks - 1
+
+    pre_copy = pltpu.make_async_copy(pre_ref, prev, pre_sem)
+    pre_copy.start()
+
+    def w_copy(k):
+        cols = pl.ds(pl.multiple_of(k * KC, KC), KC)
+        return pltpu.make_async_copy(w_ref.at[:, :, cols], wv.at[k], w_sem.at[k])
+
+    def x_src(c):
+        return x_ref.at[:, pl.ds(pl.multiple_of(c * KC, KC), KC)]
+
+    def at(zz, xx, h, c):
+        return buf.at[zz, h, c, pl.ds(pl.multiple_of(xx * 128, 128), 128), :]
+
+    def loc_copy(c):
+        return pltpu.make_async_copy(x_src(c), at(z, x, t, c), loc_sem.at[c])
+
+    @pl.loop(0, chunks)
+    def _(c):
+        loc_copy(c).start()
+
+    @pl.loop(0, 2 * chunks)
+    def _(k):
+        w_copy(k).start()
+
+    code = eid_ref[...] * slots + me * cap + slot_ref[...]
+    mine = jnp.concatenate(
+        [code.astype(jnp.float32), gate_ref[...].astype(jnp.float32)], axis=0
+    )
+    mysend[...] = mine
+    meta[me] = mine
+
+    barrier = pltpu.get_barrier_semaphore()
+    n = NZ * NX * 2
+
+    @pl.loop(0, n)
+    def _(j):
+        @pl.when(j != me * 2 + t)
+        def _():
+            pl.semaphore_signal(
+                barrier, inc=1, device_id={"ep": j // 2, "tp": j % 2}, device_id_type=MESH
+            )
+
+    pl.semaphore_wait(barrier, n - 1)
+
+    def m_copy(j):
+        return pltpu.make_async_remote_copy(
+            src_ref=mysend, dst_ref=meta.at[me], send_sem=m_send.at[j],
+            recv_sem=m_recv.at[me], device_id={"ep": j}, device_id_type=MESH,
+        )
+
+    @pl.loop(0, NZ * NX)
+    def _(j):
+        @pl.when(j != me)
+        def _():
+            m_copy(j).start()
+
+    def along_z(zz, xx, c, up, src=None):
+        b = zz * NX + xx
+        d = 1 if up else 0
+        to = me + NX if up else me - NX
+        ref = at(zz, xx, t, c)
+        return pltpu.make_async_remote_copy(
+            src_ref=ref if src is None else src, dst_ref=ref,
+            send_sem=z_send.at[d, b, c], recv_sem=own_recv.at[b, c],
+            device_id={"ep": to}, device_id_type=MESH,
+        )
+
+    def along_x(zz, c, src=None):
+        b = zz * NX + x
+        ref = at(zz, x, t, c)
+        return pltpu.make_async_remote_copy(
+            src_ref=ref if src is None else src, dst_ref=ref,
+            send_sem=x_send.at[zz, c], recv_sem=own_recv.at[b, c],
+            device_id={"ep": z * NX + oz}, device_id_type=MESH,
+        )
+
+    def to_core(zz, xx, c, src=None):
+        b = zz * NX + xx
+        ref = at(zz, xx, t, c)
+        return pltpu.make_async_remote_copy(
+            src_ref=ref if src is None else src, dst_ref=ref,
+            send_sem=tp_send.at[b, c], recv_sem=tp_recv.at[b, c],
+            device_id={"tp": 1 - t}, device_id_type=MESH,
+        )
+
+    def arrived(zz, xx, c):
+        b = zz * NX + xx
+        ref = at(zz, xx, t, c)
+        pltpu.make_async_copy(ref, ref, own_recv.at[b, c]).wait()
+
+    def core_arrived(zz, xx, c):
+        b = zz * NX + xx
+        ref = at(zz, xx, 1 - t, c)
+        pltpu.make_async_copy(ref, ref, tp_recv.at[b, c]).wait()
+
+    def order(p):
+        inner = jnp.where(p == 0, 1, jnp.where(p == 1, 2, jnp.where(p == 2, 0, 3)))
+        low = jnp.where(jnp.logical_or(z == 0, z == NZ - 1), p, inner)
+        return jnp.where(z < NZ // 2, low, NZ - 1 - low)
+
+    def chunk(i):
+        return lax.rem(i + last, chunks)
+
+    @pl.loop(0, chunks)
+    def _(i):
+        c = chunk(i)
+        along_x(z, c, x_src(c)).start()
+
+        @pl.when(z < NZ - 1)
+        def _():
+            along_z(z, x, c, True, x_src(c)).start()
+
+        @pl.when(z > 0)
+        def _():
+            along_z(z, x, c, False, x_src(c)).start()
+
+        to_core(z, x, c, x_src(c)).start()
+
+    pre_copy.wait()
+
+    @pl.loop(0, chunks)
+    def _(c):
+        loc_copy(c).wait()
+
+    @pl.loop(0, NZ * NX)
+    def _(j):
+        @pl.when(j != me)
+        def _():
+            pltpu.make_async_copy(meta.at[j], meta.at[j], m_recv.at[j]).wait()
+
+    @pl.loop(0, 2 * chunks)
+    def _(k):
+        w_copy(k).wait()
+
+    def from_row(zz, xx, c, up):
+        arrived(zz, xx, c)
+        if up:
+            @pl.when(z < NZ - 1)
+            def _():
+                along_z(zz, xx, c, True).start()
+        else:
+            @pl.when(z > 0)
+            def _():
+                along_z(zz, xx, c, False).start()
+        to_core(zz, xx, c).start()
+
+    def r_copy(p, xx, tt):
+        return pltpu.make_async_remote_copy(
+            src_ref=rsend.at[p, xx], dst_ref=rrecv.at[me * 2 + t],
+            send_sem=r_send.at[p, xx, tt], recv_sem=r_recv.at[me * 2 + t],
+            device_id={"ep": order(p) * NX + xx, "tp": tt}, device_id_type=MESH,
+        )
+
+    def out_copy(p, e):
+        rows = pl.ds(pl.multiple_of((e * NZ + order(p)) * unit, unit), unit)
+        return pltpu.make_async_copy(outv.at[rows, :], out_ref.at[rows, :], out_sem.at[p, e])
+
+    first_expert = me * experts
+
+    @pl.loop(0, NZ)
+    def _(p):
+        q = order(p)
+        nxt = order(jnp.minimum(p + 1, NZ - 1))
+        gates = []
+        for e in range(experts):
+            rows = pl.ds(pl.multiple_of((e * NZ + q) * unit, unit), unit)
+            tmp[...] = prev[rows, :].astype(jnp.float32)
+            for cb in range(cbs):
+                cols = slice(cb * 128, (cb + 1) * 128)
+                a = tmp[pl.ds(cb * 2, m, stride=per), :]
+                b = tmp[pl.ds(cb * 2 + 1, m, stride=per), :]
+                g = jax.nn.sigmoid(a)
+                act = a * g
+                coef[e, 0, 0:m, cols] = act * b
+                coef[e, 1, 0:m, cols] = b * g * (1.0 + a * (1.0 - g))
+                coef[e, 2, 0:m, cols] = act
+            base = (first_expert + e) * slots + q * m
+            want = (lax.broadcasted_iota(jnp.int32, (mp, 128), 0) + base).astype(jnp.float32)
+            gate = jnp.zeros((mp, 1), jnp.float32)
+            for xx in range(NX):
+                table = meta[q * NX + xx]
+                weight = jnp.zeros((mp, 128), jnp.float32)
+                hit = jnp.zeros((mp, 128), jnp.float32)
+                for k in range(8):
+                    same = table[k : k + 1, :] == want
+                    hit = jnp.where(same, 1.0, hit)
+                    weight = jnp.where(same, table[8 + k : 9 + k, :], weight)
+                onehot[e, :, xx * 128 : (xx + 1) * 128] = hit.astype(jnp.bfloat16)
+                gate = gate + jnp.sum(weight, axis=1, keepdims=True)
+            gates.append(gate)
+        grad[...] = jnp.zeros_like(grad)
+
+        @pl.loop(0, chunks)
+        def _(i):
+            c = chunk(i)
+
+            @pl.when(z - p - 1 >= 0)
+            def _():
+                from_row(z - p - 1, x, c, True)
+
+                @pl.when(i == last)
+                def _():
+                    from_row(z - p - 1, oz, last, True)
+
+            @pl.when(z + p + 1 < NZ)
+            def _():
+                from_row(z + p + 1, x, c, False)
+
+                @pl.when(i == last)
+                def _():
+                    from_row(z + p + 1, oz, last, False)
+
+            @pl.when(jnp.logical_and(p < NZ - 1, c < last))
+            def _():
+                along_x(nxt, c).start()
+
+            @pl.when(jnp.logical_or(p == 0, c < last))
+            def _():
+                arrived(q, oz, c)
+                to_core(q, oz, c).start()
+
+            @pl.when(jnp.logical_and(p == 0, c == last))
+            def _():
+                @pl.when(z < NZ - 1)
+                def _():
+                    along_z(z, oz, c, True).start()
+
+                @pl.when(z > 0)
+                def _():
+                    along_z(z, oz, c, False).start()
+
+            core_arrived(q, x, c)
+            core_arrived(q, oz, c)
+            picks = onehot[...].reshape(experts * mp, NX * 128)
+            total = [grad[e] for e in range(experts)]
+            for h in range(2):
+                rows = jnp.dot(
+                    picks, buf[q, h, c], preferred_element_type=jnp.float32
+                ).astype(jnp.bfloat16)
+                for e in range(experts):
+                    total[e] = total[e] + lax.dot_general(
+                        rows[e * mp : (e + 1) * mp], wv[h * chunks + c, e],
+                        (((1,), (1,)), ((), ())), preferred_element_type=jnp.float32,
+                    )
+            for e in range(experts):
+                grad[e] = total[e]
+
+        sub = lax.broadcasted_iota(jnp.int32, (8, NX * 128), 0)
+        back = jnp.zeros((8, NX * 128), jnp.float32)
+        for e in range(experts):
+            sums = jnp.zeros((m, 1), jnp.float32)
+            for cb in range(cbs):
+                cols = slice(cb * 128, (cb + 1) * 128)
+                gh = grad[e, 0:m, cols]
+                sums = sums + jnp.sum(coef[e, 0, 0:m, cols] * gh, axis=1, keepdims=True)
+                scaled = gates[e][0:m] * gh
+                tmp[pl.ds(cb * 2, m, stride=per), :] = scaled * coef[e, 1, 0:m, cols]
+                tmp[pl.ds(cb * 2 + 1, m, stride=per), :] = scaled * coef[e, 2, 0:m, cols]
+            picked = onehot[e].astype(jnp.float32)[0:m] * sums
+            row = jnp.sum(picked, axis=0, keepdims=True)
+            back = jnp.where(sub == e, row, back)
+            rows = pl.ds(pl.multiple_of((e * NZ + q) * unit, unit), unit)
+            outv[rows, :] = tmp[...].astype(jnp.bfloat16)
+            out_copy(p, e).start()
+        for xx in range(NX):
+            rsend[p, xx] = back[:, xx * 128 : (xx + 1) * 128]
+            for tt in range(2):
+                own = jnp.logical_and(q * NX + xx == me, t == tt)
+
+                @pl.when(own)
+                def _():
+                    rrecv[me * 2 + t] = back[:, xx * 128 : (xx + 1) * 128]
+
+                @pl.when(jnp.logical_not(own))
+                def _():
+                    r_copy(p, xx, tt).start()
+
+    @pl.loop(0, NZ * NX)
+    def _(j):
+        @pl.when(j != me)
+        def _():
+            m_copy(j).wait_send()
+
+    @pl.loop(0, chunks)
+    def _(i):
+        c = chunk(i)
+        along_x(z, c).wait_send()
+
+        @pl.when(z < NZ - 1)
+        def _():
+            along_z(z, x, c, True).wait_send()
+
+        @pl.when(z > 0)
+        def _():
+            along_z(z, x, c, False).wait_send()
+
+        to_core(z, x, c).wait_send()
+
+    @pl.when(z < NZ - 1)
+    def _():
+        along_z(z, oz, last, True).wait_send()
+
+    @pl.when(z > 0)
+    def _():
+        along_z(z, oz, last, False).wait_send()
+
+    def sent_row(zz, xx, c, up):
+        if up:
+            @pl.when(z < NZ - 1)
+            def _():
+                along_z(zz, xx, c, True).wait_send()
+        else:
+            @pl.when(z > 0)
+            def _():
+                along_z(zz, xx, c, False).wait_send()
+        to_core(zz, xx, c).wait_send()
+
+    @pl.loop(0, NZ)
+    def _(p):
+        q = order(p)
+        nxt = order(jnp.minimum(p + 1, NZ - 1))
+
+        @pl.loop(0, chunks)
+        def _(i):
+            c = chunk(i)
+
+            @pl.when(z - p - 1 >= 0)
+            def _():
+                sent_row(z - p - 1, x, c, True)
+
+                @pl.when(i == last)
+                def _():
+                    sent_row(z - p - 1, oz, last, True)
+
+            @pl.when(z + p + 1 < NZ)
+            def _():
+                sent_row(z + p + 1, x, c, False)
+
+                @pl.when(i == last)
+                def _():
+                    sent_row(z + p + 1, oz, last, False)
+
+            @pl.when(jnp.logical_and(p < NZ - 1, c < last))
+            def _():
+                along_x(nxt, c).wait_send()
+
+            @pl.when(jnp.logical_or(p == 0, c < last))
+            def _():
+                to_core(q, oz, c).wait_send()
+
+        for e in range(experts):
+            out_copy(p, e).wait()
+        for xx in range(NX):
+            for tt in range(2):
+                @pl.when(jnp.logical_not(jnp.logical_and(q * NX + xx == me, t == tt)))
+                def _():
+                    r_copy(p, xx, tt).wait_send()
+
+    @pl.loop(0, n)
+    def _(j):
+        @pl.when(j != me * 2 + t)
+        def _():
+            pltpu.make_async_copy(rrecv.at[j], rrecv.at[j], r_recv.at[j]).wait()
+
+    ids = eid_ref[...]
+    result = jnp.zeros(ids.shape, jnp.float32)
+    for owner in range(NZ * NX):
+        both = rrecv[owner * 2] + rrecv[owner * 2 + 1]
+        for e in range(experts):
+            result = jnp.where(ids == owner * experts + e, both[e : e + 1, :], result)
+    gg_ref[...] = result
+
+
+def relayed(cotangent, gate_weights, expert_ids, slot_ids, pre_acts, w_down):
+    experts, slots, _, hid = pre_acts.shape
+    peers = lax.axis_size("ep")
+    cap = slots // peers
+    chunks = cotangent.shape[1] // KC
+    chosen = expert_ids.shape[1]
+    cbs = hid // 128
+    m = NX * cap
+    mp = -(-m // 16) * 16
+    unit = m * 2 * cbs
+    rows = experts * slots * 2 * cbs
+    pre = pre_acts.reshape(experts, slots, 2, cbs, 128).transpose(0, 1, 3, 2, 4).reshape(rows, 128)
+    vmem = pl.BlockSpec(memory_space=pltpu.VMEM)
+    hbm = pl.BlockSpec(memory_space=pl.ANY)
+    dma = pltpu.SemaphoreType.DMA
+    bf, f32 = jnp.bfloat16, jnp.float32
+    out, gg = pl.pallas_call(
+        functools.partial(kernel, (experts, slots, cap, hid, chunks)),
+        out_shape=(
+            jax.ShapeDtypeStruct((rows, 128), bf),
+            jax.ShapeDtypeStruct((chosen, 128), f32),
+        ),
+        in_specs=[hbm, vmem, vmem, vmem, hbm, hbm],
+        out_specs=(hbm, vmem),
+        scratch_shapes=[
+            pltpu.VMEM((NZ, 2, chunks, NX * 128, KC), bf),
+            pltpu.VMEM((2 * chunks, experts, hid, KC), bf),
+            pltpu.VMEM((rows, 128), bf),
+            pltpu.VMEM((rows, 128), bf),
+            pltpu.VMEM((unit, 128), f32),
+            pltpu.VMEM((experts, 3, mp, hid), f32),
+            pltpu.VMEM((experts, mp, hid), f32),
+            pltpu.VMEM((experts, mp, NX * 128), bf),
+            pltpu.VMEM((peers, 2 * chosen, 128), f32),
+            pltpu.VMEM((2 * chosen, 128), f32),
+            pltpu.VMEM((NZ, NX, 8, 128), f32),
+            pltpu.VMEM((2 * peers, 8, 128), f32),
+            dma((peers, chunks)),
+            dma((peers, chunks)),
+            dma((2, peers, chunks)),
+            dma((NZ, chunks)),
+            dma((peers, chunks)),
+            dma((chunks,)),
+            dma((2 * chunks,)),
+            dma,
+            dma((NZ, experts)),
+            dma((peers,)),
+            dma((peers,)),
+            dma((NZ, NX, 2)),
+            dma((2 * peers,)),
+        ],
+        compiler_params=pltpu.CompilerParams(
+            collective_id=0, has_side_effects=True, vmem_limit_bytes=50 * 2**20
+        ),
+    )(cotangent, expert_ids.T, slot_ids.T, gate_weights.T, pre, w_down)
+    grad_pre = (
+        out.reshape(experts, slots, cbs, 2, 128)
+        .transpose(0, 1, 3, 2, 4)
+        .reshape(experts, slots, 2, hid)
+    )
+    return grad_pre, gg.T
+
+
+def shards(cotangent, gate_weights, expert_ids, slot_ids, pre_acts, w_down):
+    peers = lax.axis_size("ep")
+    experts, slots, _, hid = pre_acts.shape
+    tokens, chosen = expert_ids.shape
+    fits = (
+        peers == NZ * NX
+        and lax.axis_size("tp") == 2
+        and experts * (slots // peers) >= tokens
+        and experts <= 8
+        and tokens == 128
+        and chosen == 8
+        and cotangent.shape[1] % KC == 0
+        and hid % 128 == 0
+    )
+    run = relayed if fits else slotted
+    return run(cotangent, gate_weights, expert_ids, slot_ids, pre_acts, w_down)
+
+
 def solution(mesh):
     placed = (
         P(("grp", "ep"), "tp"),

time: 181 us -> 76.5 us (0.42)
  blocking collectives: 94.5 us -> 0 us
  Pallas kernels: 0 us -> 70.5 us
  local copies, waits for them, and re-layouts: 46.4 us -> 5 us
  between operations: 14.2 us -> 0.65 us
  matrix products: 11.7 us -> 0 us
  starting transfers between devices: 8.33 us -> 0 us
  waiting for transfers between devices: 4.47 us -> 0 us
    all_to_all x1 -> x0, blocking collectives: 92 us -> none  [shards(): lax.all_to_all(padded[filler // chosen].reshape(experts_here, peers, capa...]
    pallas_call x0 -> x1, Pallas kernels: none -> 70.5 us  [relayed(): pl.pallas_call(functools.partial(kernel, (experts, slots, cap, hid, chunk...]
    gather x4 -> x0, local copies, waits for them, and re-layouts: 18.7 us -> none  [the longest x1 6.92 us: shards(): send_gate = padded_gate[filler].reshape(experts_here, peers, capacity)]
    reshape x8 -> x0, local copies, waits for them, and re-layouts: 12.1 us -> none  [the longest x2 11 us: shards(): padded[filler // chosen]]
    dot_general x1 -> x0, matrix products: 11.7 us -> none  [shards(): jnp.einsum('esd,ehd->esh', arrived, w_down, preferred_element_type=jnp.fl...]
    all_to_all x2 -> x0, starting transfers between devices: 8.29 us -> none  [the longest x1 4.8 us: shards(): lax.all_to_all(summed, 'ep', split_axis=1, concat_axis=1, tiled=True)]
    all_to_all x2 -> x0, waiting for transfers between devices: 4.44 us -> none  [the longest x1 2.75 us: shards(): lax.all_to_all(summed, 'ep', split_axis=1, concat_axis=1, tiled=True)]
    scatter x1 -> x0, local copies, waits for them, and re-layouts: 4.32 us -> none  [shards(): filler = jnp.full((experts_here * slot_rows,), tok_rows * chosen, jnp.int...]
  transfers between devices with their start and end apart: 3 -> 0, of which waited for: 2 -> 0; matrix products, arithmetic and copies ran while one was open for 9% -> 0% of each run, Pallas kernels for 0% -> 0%
where the time goes in v1:
time: 76.5 us; the launch traced here: 76.2 us
  Pallas kernels  70.5 us (92%)
  local copies, waits for them, and re-layouts  5 us (7%)
    pallas_call x1, Pallas kernels, relayed(): pl.pallas_call(functools.partial(kernel, (experts, slots, cap, hid, chunk...  70.5 us
    unnamed x10, local copies, waits for them, and re-layouts  5 us

profile of v1, /device:TPU:0, one launch (start us, length us, event | category | flops | bytes accessed | tf_op | source)
XLA Modules:
  0.0 76.2 jit_solution(15298861673366068542)
XLA Ops:
  0.6 0.0 copy-start
  0.6 1.0 %copy-done = bf16[128,1792]{1,0:T(8,128)(2,1)S(1)} copy-done((bf16[128,1792]{1,0:T(8,128)(2,1)S(1)}, bf16[128,1792]{1,0:T(8,128)(2,1)}, u32[]{:S(2)}) %copy-start) | copy-done | bytes 458776
  1.7 0.0 copy-start.1
  1.7 0.7 copy-done.1
  2.3 0.0 copy-start.2
  2.3 0.7 copy-done.2
  3.0 0.0 copy-start.3
  3.0 0.7 copy-done.3
  3.7 70.5 %shard_map.77 = (bf16[8448,128]{1,0:T(8,128)(2,1)S(1)}, f32[8,128]{1,0:T(8,128)S(1)}) custom-call(bf16[128,1792]{1,0:T(8,128)(2,1)S(1)} %copy-done, s32[8,128]{1,0:T(8,128)S(1)} %bitcast.15, s32[8,128]{1,0:T(8,128)S(1)} %bitcast.16, bf16[8,128]{1,0:T(8,128)(2,1)S(1)} %bitcast.18, bf16[8448,128]{1,0:T(8,128)(2,1)} %bitcast.19, bf16[2,512,3584]{2,1,0:T(8,128)(2,1)} %w_ref.1), custom_call_target="tpu_custom_call" | custom-call | tf_op jit(solution)/shard_map/pallas_call | solution.py:473
  74.3 1.3 %copy.12 = bf16[2,528,2,512]{3,2,1,0:T(2,128)(2,1)} copy(bf16[2,528,2,512]{3,2,1,0:T(2,128)(2,1)S(1)} %bitcast.14) | data formatting | bytes 4325376
  75.6 0.6 copy.13
Async XLA Ops:
  0.6 1.0 %copy-start = (bf16[128,1792]{1,0:T(8,128)(2,1)S(1)}, bf16[128,1792]{1,0:T(8,128)(2,1)}, u32[]{:S(2)}) copy-start(bf16[128,1792]{1,0:T(8,128)(2,1)} %x_ref.1) | copy-start | bytes 1376260
  1.7 0.7 copy-start.1
  2.3 0.7 copy-start.2
  3.0 0.7 copy-start.3

commit v2 on v1

--- a/solution.py
+++ b/solution.py
@@ -9,6 +9,7 @@
 
 MESH = pl.DeviceIdType.MESH
 KC = 256
+LAG = 2
 NZ, NX = 4, 2
 
 
@@ -63,10 +64,11 @@
 
 def kernel(
     dims,
-    x_ref, eid_ref, slot_ref, gate_ref, pre_ref, w_ref,
+    x_ref, eid_hbm, slot_hbm, gate_hbm, pre_ref, w_ref,
     out_ref, gg_ref,
-    buf, wv, prev, outv, tmp, coef, grad, onehot, meta, mysend, rsend, rrecv,
-    own_recv, tp_recv, z_send, x_send, tp_send, loc_sem, w_sem, pre_sem, out_sem,
+    eid_ref, slot_ref, gate_ref,
+    buf, wv, prev, tmp, coef, grad, onehot, gates, meta, mysend, rsend, rrecv,
+    own_recv, tp_recv, z_send, x_send, tp_send, loc_sem, w_sem, pre_sem, in_sem,
     m_send, m_recv, r_send, r_recv,
 ):
     experts, slots, cap, hid, chunks = dims
@@ -81,6 +83,14 @@
     oz = 1 - x
     last = chunks - 1
 
+    small = [
+        pltpu.make_async_copy(src, dst, in_sem.at[i])
+        for i, (src, dst) in enumerate(
+            [(eid_hbm, eid_ref), (slot_hbm, slot_ref), (gate_hbm, gate_ref)]
+        )
+    ]
+    for copy in small:
+        copy.start()
     pre_copy = pltpu.make_async_copy(pre_ref, prev, pre_sem)
     pre_copy.start()
 
@@ -105,24 +115,25 @@
     def _(k):
         w_copy(k).start()
 
+    barrier = pltpu.get_barrier_semaphore()
+    n = NZ * NX * 2
+
+    @pl.loop(0, n)
+    def _(j):
+        @pl.when(j != me * 2 + t)
+        def _():
+            pl.semaphore_signal(
+                barrier, inc=1, device_id={"ep": j // 2, "tp": j % 2}, device_id_type=MESH
+            )
+
+    for copy in small:
+        copy.wait()
     code = eid_ref[...] * slots + me * cap + slot_ref[...]
     mine = jnp.concatenate(
         [code.astype(jnp.float32), gate_ref[...].astype(jnp.float32)], axis=0
     )
     mysend[...] = mine
     meta[me] = mine
-
-    barrier = pltpu.get_barrier_semaphore()
-    n = NZ * NX * 2
-
-    @pl.loop(0, n)
-    def _(j):
-        @pl.when(j != me * 2 + t)
-        def _():
-            pl.semaphore_signal(
-                barrier, inc=1, device_id={"ep": j // 2, "tp": j % 2}, device_id_type=MESH
-            )
-
     pl.semaphore_wait(barrier, n - 1)
 
     def m_copy(j):
@@ -130,12 +141,6 @@
             src_ref=mysend, dst_ref=meta.at[me], send_sem=m_send.at[j],
             recv_sem=m_recv.at[me], device_id={"ep": j}, device_id_type=MESH,
         )
-
-    @pl.loop(0, NZ * NX)
-    def _(j):
-        @pl.when(j != me)
-        def _():
-            m_copy(j).start()
 
     def along_z(zz, xx, c, up, src=None):
         b = zz * NX + xx
@@ -144,7 +149,7 @@
         ref = at(zz, xx, t, c)
         return pltpu.make_async_remote_copy(
             src_ref=ref if src is None else src, dst_ref=ref,
-            send_sem=z_send.at[d, b, c], recv_sem=own_recv.at[b, c],
+            send_sem=z_send.at[d, b], recv_sem=own_recv.at[b, c],
             device_id={"ep": to}, device_id_type=MESH,
         )
 
@@ -153,7 +158,7 @@
         ref = at(zz, x, t, c)
         return pltpu.make_async_remote_copy(
             src_ref=ref if src is None else src, dst_ref=ref,
-            send_sem=x_send.at[zz, c], recv_sem=own_recv.at[b, c],
+            send_sem=x_send.at[zz], recv_sem=own_recv.at[b, c],
             device_id={"ep": z * NX + oz}, device_id_type=MESH,
         )
 
@@ -162,9 +167,15 @@
         ref = at(zz, xx, t, c)
         return pltpu.make_async_remote_copy(
             src_ref=ref if src is None else src, dst_ref=ref,
-            send_sem=tp_send.at[b, c], recv_sem=tp_recv.at[b, c],
+            send_sem=tp_send.at[b], recv_sem=tp_recv.at[b, c],
             device_id={"tp": 1 - t}, device_id_type=MESH,
         )
+
+    @pl.loop(0, NZ * NX)
+    def _(j):
+        @pl.when(j != me)
+        def _():
+            m_copy(j).start()
 
     def arrived(zz, xx, c):
         b = zz * NX + xx
@@ -234,17 +245,51 @@
             device_id={"ep": order(p) * NX + xx, "tp": tt}, device_id_type=MESH,
         )
 
-    def out_copy(p, e):
-        rows = pl.ds(pl.multiple_of((e * NZ + order(p)) * unit, unit), unit)
-        return pltpu.make_async_copy(outv.at[rows, :], out_ref.at[rows, :], out_sem.at[p, e])
-
     first_expert = me * experts
 
-    @pl.loop(0, NZ)
-    def _(p):
+    def carry(s):
+        p, i = s // chunks, lax.rem(s, chunks)
+        c = chunk(i)
         q = order(p)
         nxt = order(jnp.minimum(p + 1, NZ - 1))
-        gates = []
+
+        @pl.when(z - p - 1 >= 0)
+        def _():
+            from_row(z - p - 1, x, c, True)
+
+            @pl.when(i == last)
+            def _():
+                from_row(z - p - 1, oz, last, True)
+
+        @pl.when(z + p + 1 < NZ)
+        def _():
+            from_row(z + p + 1, x, c, False)
+
+            @pl.when(i == last)
+            def _():
+                from_row(z + p + 1, oz, last, False)
+
+        @pl.when(jnp.logical_and(p < NZ - 1, c < last))
+        def _():
+            along_x(nxt, c).start()
+
+        @pl.when(jnp.logical_or(p == 0, c < last))
+        def _():
+            arrived(q, oz, c)
+            to_core(q, oz, c).start()
+
+        @pl.when(jnp.logical_and(p == 0, c == last))
+        def _():
+            @pl.when(z < NZ - 1)
+            def _():
+                along_z(z, oz, c, True).start()
+
+            @pl.when(z > 0)
+            def _():
+                along_z(z, oz, c, False).start()
+
+    def prepare(p):
+        q = order(p)
         for e in range(experts):
             rows = pl.ds(pl.multiple_of((e * NZ + q) * unit, unit), unit)
             tmp[...] = prev[rows, :].astype(jnp.float32)
@@ -270,64 +315,29 @@
                     weight = jnp.where(same, table[8 + k : 9 + k, :], weight)
                 onehot[e, :, xx * 128 : (xx + 1) * 128] = hit.astype(jnp.bfloat16)
                 gate = gate + jnp.sum(weight, axis=1, keepdims=True)
-            gates.append(gate)
+            gates[e] = jnp.broadcast_to(gate, (mp, 128))
         grad[...] = jnp.zeros_like(grad)
 
-        @pl.loop(0, chunks)
-        def _(i):
-            c = chunk(i)
-
-            @pl.when(z - p - 1 >= 0)
-            def _():
-                from_row(z - p - 1, x, c, True)
-
-                @pl.when(i == last)
-                def _():
-                    from_row(z - p - 1, oz, last, True)
-
-            @pl.when(z + p + 1 < NZ)
-            def _():
-                from_row(z + p + 1, x, c, False)
-
-                @pl.when(i == last)
-                def _():
-                    from_row(z + p + 1, oz, last, False)
-
-            @pl.when(jnp.logical_and(p < NZ - 1, c < last))
-            def _():
-                along_x(nxt, c).start()
-
-            @pl.when(jnp.logical_or(p == 0, c < last))
-            def _():
-                arrived(q, oz, c)
-                to_core(q, oz, c).start()
-
-            @pl.when(jnp.logical_and(p == 0, c == last))
-            def _():
-                @pl.when(z < NZ - 1)
-                def _():
-                    along_z(z, oz, c, True).start()
-
-                @pl.when(z > 0)
-                def _():
-                    along_z(z, oz, c, False).start()
-
-            core_arrived(q, x, c)
-            core_arrived(q, oz, c)
-            picks = onehot[...].reshape(experts * mp, NX * 128)
-            total = [grad[e] for e in range(experts)]
-            for h in range(2):
-                rows = jnp.dot(
-                    picks, buf[q, h, c], preferred_element_type=jnp.float32
-                ).astype(jnp.bfloat16)
-                for e in range(experts):
-                    total[e] = total[e] + lax.dot_general(
-                        rows[e * mp : (e + 1) * mp], wv[h * chunks + c, e],
-                        (((1,), (1,)), ((), ())), preferred_element_type=jnp.float32,
-                    )
+    def multiply(p, c):
+        q = order(p)
+        core_arrived(q, x, c)
+        core_arrived(q, oz, c)
+        picks = onehot[...].reshape(experts * mp, NX * 128)
+        total = [grad[e] for e in range(experts)]
+        for h in range(2):
+            rows = jnp.dot(
+                picks, buf[q, h, c], preferred_element_type=jnp.float32
+            ).astype(jnp.bfloat16)
             for e in range(experts):
-                grad[e] = total[e]
-
+                total[e] = total[e] + lax.dot_general(
+                    rows[e * mp : (e + 1) * mp], wv[h * chunks + c, e],
+                    (((1,), (1,)), ((), ())), preferred_element_type=jnp.float32,
+                )
+        for e in range(experts):
+            grad[e] = total[e]
+
+    def finish(p):
+        q = order(p)
         sub = lax.broadcasted_iota(jnp.int32, (8, NX * 128), 0)
         back = jnp.zeros((8, NX * 128), jnp.float32)
         for e in range(experts):
@@ -336,15 +346,14 @@
                 cols = slice(cb * 128, (cb + 1) * 128)
                 gh = grad[e, 0:m, cols]
                 sums = sums + jnp.sum(coef[e, 0, 0:m, cols] * gh, axis=1, keepdims=True)
-                scaled = gates[e][0:m] * gh
+                scaled = gates[e, 0:m, :] * gh
                 tmp[pl.ds(cb * 2, m, stride=per), :] = scaled * coef[e, 1, 0:m, cols]
                 tmp[pl.ds(cb * 2 + 1, m, stride=per), :] = scaled * coef[e, 2, 0:m, cols]
             picked = onehot[e].astype(jnp.float32)[0:m] * sums
             row = jnp.sum(picked, axis=0, keepdims=True)
             back = jnp.where(sub == e, row, back)
             rows = pl.ds(pl.multiple_of((e * NZ + q) * unit, unit), unit)
-            outv[rows, :] = tmp[...].astype(jnp.bfloat16)
-            out_copy(p, e).start()
+            out_ref[rows, :] = tmp[...].astype(jnp.bfloat16)
         for xx in range(NX):
             rsend[p, xx] = back[:, xx * 128 : (xx + 1) * 128]
             for tt in range(2):
@@ -358,86 +367,64 @@
                 def _():
                     r_copy(p, xx, tt).start()
 
+    @pl.loop(0, NZ * chunks + LAG)
+    def _(s):
+        @pl.when(s < NZ * chunks)
+        def _():
+            carry(s)
+
+        @pl.when(s >= LAG)
+        def _():
+            p, i = (s - LAG) // chunks, lax.rem(s - LAG, chunks)
+
+            @pl.when(i == 0)
+            def _():
+                prepare(p)
+
+            multiply(p, chunk(i))
+
+            @pl.when(i == last)
+            def _():
+                finish(p)
+
     @pl.loop(0, NZ * NX)
     def _(j):
         @pl.when(j != me)
         def _():
             m_copy(j).wait_send()
 
-    @pl.loop(0, chunks)
-    def _(i):
-        c = chunk(i)
-        along_x(z, c).wait_send()
-
-        @pl.when(z < NZ - 1)
-        def _():
-            along_z(z, x, c, True).wait_send()
-
-        @pl.when(z > 0)
-        def _():
-            along_z(z, x, c, False).wait_send()
-
-        to_core(z, x, c).wait_send()
-
-    @pl.when(z < NZ - 1)
-    def _():
-        along_z(z, oz, last, True).wait_send()
-
-    @pl.when(z > 0)
-    def _():
-        along_z(z, oz, last, False).wait_send()
-
-    def sent_row(zz, xx, c, up):
-        if up:
-            @pl.when(z < NZ - 1)
-            def _():
-                along_z(zz, xx, c, True).wait_send()
-        else:
-            @pl.when(z > 0)
-            def _():
-                along_z(zz, xx, c, False).wait_send()
-        to_core(zz, xx, c).wait_send()
+    def sent(sem, zz, xx, count):
+        ref = buf.at[zz, t, 0:count, pl.ds(pl.multiple_of(xx * 128, 128), 128), :]
+        pltpu.make_async_copy(ref, ref, sem).wait()
 
     @pl.loop(0, NZ)
-    def _(p):
-        q = order(p)
-        nxt = order(jnp.minimum(p + 1, NZ - 1))
-
-        @pl.loop(0, chunks)
-        def _(i):
-            c = chunk(i)
-
-            @pl.when(z - p - 1 >= 0)
-            def _():
-                sent_row(z - p - 1, x, c, True)
-
-                @pl.when(i == last)
-                def _():
-                    sent_row(z - p - 1, oz, last, True)
-
-            @pl.when(z + p + 1 < NZ)
-            def _():
-                sent_row(z + p + 1, x, c, False)
-
-                @pl.when(i == last)
-                def _():
-                    sent_row(z + p + 1, oz, last, False)
-
-            @pl.when(jnp.logical_and(p < NZ - 1, c < last))
-            def _():
-                along_x(nxt, c).wait_send()
-
-            @pl.when(jnp.logical_or(p == 0, c < last))
-            def _():
-                to_core(q, oz, c).wait_send()
-
-        for e in range(experts):
-            out_copy(p, e).wait()
+    def _(zz):
+        for xx in range(NX):
+            sent(tp_send.at[zz * NX + xx], zz, xx, chunks)
+
+        @pl.when(zz == z)
+        def _():
+            sent(x_send.at[zz], zz, x, chunks)
+
+        @pl.when(zz != z)
+        def _():
+            sent(x_send.at[zz], zz, x, last)
+
+        @pl.when(jnp.logical_and(zz <= z, z < NZ - 1))
+        def _():
+            sent(z_send.at[1, zz * NX + x], zz, x, chunks)
+            sent(z_send.at[1, zz * NX + oz], zz, oz, 1)
+
+        @pl.when(jnp.logical_and(zz >= z, z > 0))
+        def _():
+            sent(z_send.at[0, zz * NX + x], zz, x, chunks)
+            sent(z_send.at[0, zz * NX + oz], zz, oz, 1)
+
         for xx in range(NX):
             for tt in range(2):
-                @pl.when(jnp.logical_not(jnp.logical_and(q * NX + xx == me, t == tt)))
+                @pl.when(jnp.logical_not(jnp.logical_and(order(zz) * NX + xx == me, t == tt)))
                 def _():
-                    r_copy(p, xx, tt).wait_send()
+                    r_copy(zz, xx, tt).wait_send()
 
     @pl.loop(0, n)
     def _(j):
@@ -467,7 +454,7 @@
     rows = experts * slots * 2 * cbs
     pre = pre_acts.reshape(experts, slots, 2, cbs, 128).transpose(0, 1, 3, 2, 4).reshape(rows, 128)
     vmem = pl.BlockSpec(memory_space=pltpu.VMEM)
-    hbm = pl.BlockSpec(memory_space=pl.ANY)
+    hbm = pl.BlockSpec(memory_space=pltpu.HBM)
     dma = pltpu.SemaphoreType.DMA
     bf, f32 = jnp.bfloat16, jnp.float32
     out, gg = pl.pallas_call(
@@ -476,30 +463,33 @@
             jax.ShapeDtypeStruct((rows, 128), bf),
             jax.ShapeDtypeStruct((chosen, 128), f32),
         ),
-        in_specs=[hbm, vmem, vmem, vmem, hbm, hbm],
-        out_specs=(hbm, vmem),
+        in_specs=[hbm] * 6,
+        out_specs=(vmem, vmem),
         scratch_shapes=[
+            pltpu.VMEM((chosen, 128), jnp.int32),
+            pltpu.VMEM((chosen, 128), jnp.int32),
+            pltpu.VMEM((chosen, 128), bf),
             pltpu.VMEM((NZ, 2, chunks, NX * 128, KC), bf),
             pltpu.VMEM((2 * chunks, experts, hid, KC), bf),
-            pltpu.VMEM((rows, 128), bf),
             pltpu.VMEM((rows, 128), bf),
             pltpu.VMEM((unit, 128), f32),
             pltpu.VMEM((experts, 3, mp, hid), f32),
             pltpu.VMEM((experts, mp, hid), f32),
             pltpu.VMEM((experts, mp, NX * 128), bf),
+            pltpu.VMEM((experts, mp, 128), f32),
             pltpu.VMEM((peers, 2 * chosen, 128), f32),
             pltpu.VMEM((2 * chosen, 128), f32),
             pltpu.VMEM((NZ, NX, 8, 128), f32),
             pltpu.VMEM((2 * peers, 8, 128), f32),
             dma((peers, chunks)),
             dma((peers, chunks)),
-            dma((2, peers, chunks)),
-            dma((NZ, chunks)),
-            dma((peers, chunks)),
+            dma((2, peers)),
+            dma((NZ,)),
+            dma((peers,)),
             dma((chunks,)),
             dma((2 * chunks,)),
             dma,
-            dma((NZ, experts)),
+            dma((3,)),
             dma((peers,)),
             dma((peers,)),
             dma((NZ, NX, 2)),

time: 76.5 us -> 63.3 us (0.83)
  Pallas kernels: 70.5 us -> 57.4 us
    pallas_call x1, Pallas kernels: 70.5 us -> 57.4 us  [relayed(): pl.pallas_call(functools.partial(kernel, (experts, slots, cap, hid, chunk...]
where the time goes in v2:
time: 63.3 us; the launch traced here: 63 us
  Pallas kernels  57.4 us (91%)
  local copies, waits for them, and re-layouts  5 us (8%)
  between operations  0.65 us (1%)
    pallas_call x1, Pallas kernels, relayed(): pl.pallas_call(functools.partial(kernel, (experts, slots, cap, hid, chunk...  57.4 us
    unnamed x10, local copies, waits for them, and re-layouts  5 us

profile of v2, /device:TPU:0, one launch (start us, length us, event | category | flops | bytes accessed | tf_op | source)
XLA Modules:
  0.0 63.0 jit_solution(1708143930650598577)
XLA Ops:
  0.6 0.0 copy-start
  0.6 1.0 %copy-done = bf16[128,1792]{1,0:T(8,128)(2,1)S(1)} copy-done((bf16[128,1792]{1,0:T(8,128)(2,1)S(1)}, bf16[128,1792]{1,0:T(8,128)(2,1)}, u32[]{:S(2)}) %copy-start) | copy-done | bytes 458776
  1.7 0.0 copy-start.1
  1.7 0.7 %copy-done.1 = s32[128,8]{0,1:T(8,128)S(1)} copy-done((s32[128,8]{0,1:T(8,128)S(1)}, s32[128,8]{0,1:T(8,128)}, u32[]{:S(2)}) %copy-start.1) | copy-done | bytes 4120
  2.3 0.0 copy-start.2
  2.3 0.7 %copy-done.2 = s32[128,8]{0,1:T(8,128)S(1)} copy-done((s32[128,8]{0,1:T(8,128)S(1)}, s32[128,8]{0,1:T(8,128)}, u32[]{:S(2)}) %copy-start.2) | copy-done | bytes 4120
  3.0 0.0 copy-start.3
  3.0 0.7 %copy-done.3 = bf16[128,8]{0,1:T(8,128)(2,1)S(1)} copy-done((bf16[128,8]{0,1:T(8,128)(2,1)S(1)}, bf16[128,8]{0,1:T(8,128)(2,1)}, u32[]{:S(2)}) %copy-start.3) | copy-done | bytes 2072
  3.7 57.4 %shard_map.77 = (bf16[8448,128]{1,0:T(8,128)(2,1)S(1)}, f32[8,128]{1,0:T(8,128)S(1)}) custom-call(bf16[128,1792]{1,0:T(8,128)(2,1)S(1)} %copy-done, s32[8,128]{1,0:T(8,128)S(1)} %bitcast.15, s32[8,128]{1,0:T(8,128)S(1)} %bitcast.16, bf16[8,128]{1,0:T(8,128)(2,1)S(1)} %bitcast.18, bf16[8448,128]{1,0:T(8,128)(2,1)} %bitcast.19, bf16[2,512,3584]{2,1,0:T(8,128)(2,1)} %w_ref.1), custom_call_target="tpu_custom_call" | custom-call | tf_op jit(solution)/shard_map/pallas_call | solution.py:460
  61.1 1.3 %copy.12 = bf16[2,528,2,512]{3,2,1,0:T(2,128)(2,1)} copy(bf16[2,528,2,512]{3,2,1,0:T(2,128)(2,1)S(1)} %bitcast.14) | data formatting | bytes 4325376
  62.4 0.6 copy.13
Async XLA Ops:
  0.6 1.0 %copy-start = (bf16[128,1792]{1,0:T(8,128)(2,1)S(1)}, bf16[128,1792]{1,0:T(8,128)(2,1)}, u32[]{:S(2)}) copy-start(bf16[128,1792]{1,0:T(8,128)(2,1)} %x_ref.1) | copy-start | bytes 1376260
  1.7 0.7 %copy-start.1 = (s32[128,8]{0,1:T(8,128)S(1)}, s32[128,8]{0,1:T(8,128)}, u32[]{:S(2)}) copy-start(s32[128,8]{0,1:T(8,128)} %param.8) | copy-start | bytes 12292
  2.3 0.7 %copy-start.2 = (s32[128,8]{0,1:T(8,128)S(1)}, s32[128,8]{0,1:T(8,128)}, u32[]{:S(2)}) copy-start(s32[128,8]{0,1:T(8,128)} %param.9) | copy-start | bytes 12292
  3.0 0.7 %copy-start.3 = (bf16[128,8]{0,1:T(8,128)(2,1)S(1)}, bf16[128,8]{0,1:T(8,128)(2,1)}, u32[]{:S(2)}) copy-start(bf16[128,8]{0,1:T(8,128)(2,1)} %param.7) | copy-start | bytes 6148

commit v3 on v2

--- a/solution.py
+++ b/solution.py
@@ -64,11 +64,10 @@
 
 def kernel(
     dims,
-    x_ref, eid_hbm, slot_hbm, gate_hbm, pre_ref, w_ref,
+    x_ref, table_ref, pre_ref, w_ref,
     out_ref, gg_ref,
-    eid_ref, slot_ref, gate_ref,
-    buf, wv, prev, tmp, coef, grad, onehot, gates, meta, mysend, rsend, rrecv,
-    own_recv, tp_recv, z_send, x_send, tp_send, loc_sem, w_sem, pre_sem, in_sem,
+    buf, wv, prev, tmp, coef, grad, onehot, gates, meta, rsend, rrecv,
+    own_recv, tp_recv, z_send, x_send, tp_send, loc_sem, w_sem, pre_sem,
     m_send, m_recv, r_send, r_recv,
 ):
     experts, slots, cap, hid, chunks = dims
@@ -83,14 +82,6 @@
     oz = 1 - x
     last = chunks - 1
 
-    small = [
-        pltpu.make_async_copy(src, dst, in_sem.at[i])
-        for i, (src, dst) in enumerate(
-            [(eid_hbm, eid_ref), (slot_hbm, slot_ref), (gate_hbm, gate_ref)]
-        )
-    ]
-    for copy in small:
-        copy.start()
     pre_copy = pltpu.make_async_copy(pre_ref, prev, pre_sem)
     pre_copy.start()
 
@@ -126,19 +117,12 @@
                 barrier, inc=1, device_id={"ep": j // 2, "tp": j % 2}, device_id_type=MESH
             )
 
-    for copy in small:
-        copy.wait()
-    code = eid_ref[...] * slots + me * cap + slot_ref[...]
-    mine = jnp.concatenate(
-        [code.astype(jnp.float32), gate_ref[...].astype(jnp.float32)], axis=0
-    )
-    mysend[...] = mine
-    meta[me] = mine
+    meta[me] = table_ref[...]
     pl.semaphore_wait(barrier, n - 1)
 
     def m_copy(j):
         return pltpu.make_async_remote_copy(
-            src_ref=mysend, dst_ref=meta.at[me], send_sem=m_send.at[j],
+            src_ref=table_ref, dst_ref=meta.at[me], send_sem=m_send.at[j],
             recv_sem=m_recv.at[me], device_id={"ep": j}, device_id_type=MESH,
         )
 
@@ -171,12 +155,6 @@
             device_id={"tp": 1 - t}, device_id_type=MESH,
         )
 
-    @pl.loop(0, NZ * NX)
-    def _(j):
-        @pl.when(j != me)
-        def _():
-            m_copy(j).start()
-
     def arrived(zz, xx, c):
         b = zz * NX + xx
         ref = at(zz, xx, t, c)
@@ -210,21 +188,11 @@
 
         to_core(z, x, c, x_src(c)).start()
 
-    pre_copy.wait()
-
-    @pl.loop(0, chunks)
-    def _(c):
-        loc_copy(c).wait()
-
     @pl.loop(0, NZ * NX)
     def _(j):
         @pl.when(j != me)
         def _():
-            pltpu.make_async_copy(meta.at[j], meta.at[j], m_recv.at[j]).wait()
-
-    @pl.loop(0, 2 * chunks)
-    def _(k):
-        w_copy(k).wait()
+            m_copy(j).start()
 
     def from_row(zz, xx, c, up):
         arrived(zz, xx, c)
@@ -377,6 +345,24 @@
         def _():
             p, i = (s - LAG) // chunks, lax.rem(s - LAG, chunks)
 
+            @pl.when(s == LAG)
+            def _():
+                pre_copy.wait()
+
+                @pl.loop(0, chunks)
+                def _(c):
+                    loc_copy(c).wait()
+
+                @pl.loop(0, NZ * NX)
+                def _(j):
+                    @pl.when(j != me)
+                    def _():
+                        pltpu.make_async_copy(meta.at[j], meta.at[j], m_recv.at[j]).wait()
+
+                @pl.loop(0, 2 * chunks)
+                def _(k):
+                    w_copy(k).wait()
+
             @pl.when(i == 0)
             def _():
                 prepare(p)
@@ -432,12 +418,14 @@
         def _():
             pltpu.make_async_copy(rrecv.at[j], rrecv.at[j], r_recv.at[j]).wait()
 
-    ids = eid_ref[...]
-    result = jnp.zeros(ids.shape, jnp.float32)
+    code = table_ref[0:8, :]
+    result = jnp.zeros(code.shape, jnp.float32)
     for owner in range(NZ * NX):
         both = rrecv[owner * 2] + rrecv[owner * 2 + 1]
         for e in range(experts):
-            result = jnp.where(ids == owner * experts + e, both[e : e + 1, :], result)
+            start = float((owner * experts + e) * slots)
+            here = jnp.logical_and(code >= start, code < start + slots)
+            result = jnp.where(here, both[e : e + 1, :], result)
     gg_ref[...] = result
 
 
@@ -453,6 +441,8 @@
     unit = m * 2 * cbs
     rows = experts * slots * 2 * cbs
     pre = pre_acts.reshape(experts, slots, 2, cbs, 128).transpose(0, 1, 3, 2, 4).reshape(rows, 128)
+    code = expert_ids * slots + lax.axis_index("ep") * cap + slot_ids
+    table = jnp.concatenate([code.T.astype(jnp.float32), gate_weights.T.astype(jnp.float32)])
     vmem = pl.BlockSpec(memory_space=pltpu.VMEM)
     hbm = pl.BlockSpec(memory_space=pltpu.HBM)
     dma = pltpu.SemaphoreType.DMA
@@ -463,12 +453,9 @@
             jax.ShapeDtypeStruct((rows, 128), bf),
             jax.ShapeDtypeStruct((chosen, 128), f32),
         ),
-        in_specs=[hbm] * 6,
+        in_specs=[hbm, vmem, hbm, hbm],
         out_specs=(vmem, vmem),
         scratch_shapes=[
-            pltpu.VMEM((chosen, 128), jnp.int32),
-            pltpu.VMEM((chosen, 128), jnp.int32),
-            pltpu.VMEM((chosen, 128), bf),
             pltpu.VMEM((NZ, 2, chunks, NX * 128, KC), bf),
             pltpu.VMEM((2 * chunks, experts, hid, KC), bf),
             pltpu.VMEM((rows, 128), bf),
@@ -478,7 +465,6 @@
             pltpu.VMEM((experts, mp, NX * 128), bf),
             pltpu.VMEM((experts, mp, 128), f32),
             pltpu.VMEM((peers, 2 * chosen, 128), f32),
-            pltpu.VMEM((2 * chosen, 128), f32),
             pltpu.VMEM((NZ, NX, 8, 128), f32),
             pltpu.VMEM((2 * peers, 8, 128), f32),
             dma((peers, chunks)),
@@ -489,7 +475,6 @@
             dma((chunks,)),
             dma((2 * chunks,)),
             dma,
-            dma((3,)),
             dma((peers,)),
             dma((peers,)),
             dma((NZ, NX, 2)),
@@ -498,7 +483,7 @@
         compiler_params=pltpu.CompilerParams(
             collective_id=0, has_side_effects=True, vmem_limit_bytes=50 * 2**20
         ),
-    )(cotangent, expert_ids.T, slot_ids.T, gate_weights.T, pre, w_down)
+    )(cotangent, table, pre, w_down)
     grad_pre = (
         out.reshape(experts, slots, cbs, 2, 128)
         .transpose(0, 1, 3, 2, 4)

time: 63.3 us -> 62.6 us (0.989)
  local copies, waits for them, and re-layouts: 5 us -> 2.95 us
  other arithmetic: 0 us -> 1.4 us
    unnamed x10 -> x4, local copies, waits for them, and re-layouts: 5 us -> 2.95 us
    convert_element_type x0 -> x2, other arithmetic: none -> 1.39 us  [the longest x1 0.71 us: relayed(): code.T.astype(jnp.float32)]
where the time goes in v3:
time: 62.6 us; the launch traced here: 62.3 us
  Pallas kernels  57.3 us (92%)
  local copies, waits for them, and re-layouts  2.95 us (5%)
  other arithmetic  1.4 us (2%)
  between operations  0.65 us (1%)
    pallas_call x1, Pallas kernels, relayed(): pl.pallas_call(functools.partial(kernel, (experts, slots, cap, hid, chunk...  57.3 us
    unnamed x4, local copies, waits for them, and re-layouts  2.95 us

profile of v3, /device:TPU:0, one launch (start us, length us, event | category | flops | bytes accessed | tf_op | source)
XLA Modules:
  0.0 62.3 jit_solution(11699745817909562029)
XLA Ops:
  0.6 0.7 %convert_bitcast_fusion.1 = f32[8,128]{1,0:T(8,128)S(1)} fusion(s32[128,8]{0,1:T(8,128)} %param.9, s32[128,8]{0,1:T(8,128)} %param.8, s32[]{:T(128)S(6)} %mul.11), kind=kLoop, calls=%fused_computation.2 | loop fusion | flops 4096 | bytes 12292 | tf_op jit(solution)/shard_map/convert_element_type | solution.py:445
  1.3 0.7 %convert_bitcast_fusion = f32[8,128]{1,0:T(8,128)S(1)} fusion(bf16[128,8]{0,1:T(8,128)(2,1)} %param.7), kind=kLoop, calls=%fused_computation.1 | loop fusion | flops 1024 | bytes 6144 | tf_op jit(solution)/shard_map/convert_element_type | solution.py:445
  2.0 0.0 copy-start
  2.0 1.0 %copy-done = bf16[128,1792]{1,0:T(8,128)(2,1)S(1)} copy-done((bf16[128,1792]{1,0:T(8,128)(2,1)S(1)}, bf16[128,1792]{1,0:T(8,128)(2,1)}, u32[]{:S(2)}) %copy-start) | copy-done | bytes 458776
  3.1 57.3 %shard_map.77 = (bf16[8448,128]{1,0:T(8,128)(2,1)S(1)}, f32[8,128]{1,0:T(8,128)S(1)}) custom-call(bf16[128,1792]{1,0:T(8,128)(2,1)S(1)} %copy-done, f32[16,128]{1,0:T(8,128)S(1)} %pad_maximum_fusion.table_ref, bf16[8448,128]{1,0:T(8,128)(2,1)} %bitcast.17, bf16[2,512,3584]{2,1,0:T(8,128)(2,1)} %w_ref.1), custom_call_target="tpu_custom_call" | custom-call | tf_op jit(solution)/shard_map/pallas_call | solution.py:450
  60.4 1.3 %copy.12 = bf16[2,528,2,512]{3,2,1,0:T(2,128)(2,1)} copy(bf16[2,528,2,512]{3,2,1,0:T(2,128)(2,1)S(1)} %bitcast.15) | data formatting | bytes 4325376
  61.7 0.6 copy.13
  (1 shorter events, 0.0 us)
Async XLA Ops:
  2.0 1.0 %copy-start = (bf16[128,1792]{1,0:T(8,128)(2,1)S(1)}, bf16[128,1792]{1,0:T(8,128)(2,1)}, u32[]{:S(2)}) copy-start(bf16[128,1792]{1,0:T(8,128)(2,1)} %x_ref.1) | copy-start | bytes 1376260

commit v4 on v3

--- a/solution.py
+++ b/solution.py
@@ -9,7 +9,7 @@
 
 MESH = pl.DeviceIdType.MESH
 KC = 256
-LAG = 2
+LAG = 1
 NZ, NX = 4, 2
 
 

time: 62.6 us -> 63.4 us (1.013)
  Pallas kernels: 57.3 us -> 58.1 us
    pallas_call x1, Pallas kernels: 57.3 us -> 58.1 us  [relayed(): pl.pallas_call(functools.partial(kernel, (experts, slots, cap, hid, chunk...]
where the time goes in v4:
time: 63.4 us; the launch traced here: 63.1 us
  Pallas kernels  58.1 us (92%)
  local copies, waits for them, and re-layouts  2.95 us (5%)
  other arithmetic  1.4 us (2%)
  between operations  0.65 us (1%)
    pallas_call x1, Pallas kernels, relayed(): pl.pallas_call(functools.partial(kernel, (experts, slots, cap, hid, chunk...  58.1 us
    unnamed x4, local copies, waits for them, and re-layouts  2.95 us

profile of v4, /device:TPU:0, one launch (start us, length us, event | category | flops | bytes accessed | tf_op | source)
XLA Modules:
  0.0 63.1 jit_solution(9987645679747930613)
XLA Ops:
  0.6 0.7 %convert_bitcast_fusion.1 = f32[8,128]{1,0:T(8,128)S(1)} fusion(s32[128,8]{0,1:T(8,128)} %param.9, s32[128,8]{0,1:T(8,128)} %param.8, s32[]{:T(128)S(6)} %mul.11), kind=kLoop, calls=%fused_computation.2 | loop fusion | flops 4096 | bytes 12292 | tf_op jit(solution)/shard_map/convert_element_type | solution.py:445
  1.3 0.7 %convert_bitcast_fusion = f32[8,128]{1,0:T(8,128)S(1)} fusion(bf16[128,8]{0,1:T(8,128)(2,1)} %param.7), kind=kLoop, calls=%fused_computation.1 | loop fusion | flops 1024 | bytes 6144 | tf_op jit(solution)/shard_map/convert_element_type | solution.py:445
  2.0 0.0 copy-start
  2.0 1.0 %copy-done = bf16[128,1792]{1,0:T(8,128)(2,1)S(1)} copy-done((bf16[128,1792]{1,0:T(8,128)(2,1)S(1)}, bf16[128,1792]{1,0:T(8,128)(2,1)}, u32[]{:S(2)}) %copy-start) | copy-done | bytes 458776
  3.1 58.1 %shard_map.77 = (bf16[8448,128]{1,0:T(8,128)(2,1)S(1)}, f32[8,128]{1,0:T(8,128)S(1)}) custom-call(bf16[128,1792]{1,0:T(8,128)(2,1)S(1)} %copy-done, f32[16,128]{1,0:T(8,128)S(1)} %pad_maximum_fusion.table_ref, bf16[8448,128]{1,0:T(8,128)(2,1)} %bitcast.17, bf16[2,512,3584]{2,1,0:T(8,128)(2,1)} %w_ref.1), custom_call_target="tpu_custom_call" | custom-call | tf_op jit(solution)/shard_map/pallas_call | solution.py:450
  61.2 1.3 %copy.12 = bf16[2,528,2,512]{3,2,1,0:T(2,128)(2,1)} copy(bf16[2,528,2,512]{3,2,1,0:T(2,128)(2,1)S(1)} %bitcast.15) | data formatting | bytes 4325376
  62.5 0.6 copy.13
  (1 shorter events, 0.0 us)
Async XLA Ops:
  2.0 1.0 %copy-start = (bf16[128,1792]{1,0:T(8,128)(2,1)S(1)}, bf16[128,1792]{1,0:T(8,128)(2,1)}, u32[]{:S(2)}) copy-start(bf16[128,1792]{1,0:T(8,128)(2,1)} %x_ref.1) | copy-start | bytes 1376260
